TPU v7x, 32 devices: a whole 2x2x4 slice. The times are simulated.
32 devices in a mesh: row: 4 (over y, x), col: 8 (over z, core).
Axes of the slice: x: 2, y: 2, z: 4, core: 2. Of those that a mesh axis runs over, the one named last changes fastest.
Arguments:
- value: bfloat16 [1024, 1024, 128], P('row', 'col'), may hold values from -6 to 6
- gate: bfloat16 [1024, 1024, 128], P('row', 'col'), may hold values from -6 to 6
- filter_real: float32 [1024, 1024, 128], P(None, ('row', 'col')), may hold values from -6 to 6
- filter_imag: float32 [1024, 1024, 128], P(None, ('row', 'col')), may hold values from -6 to 6
- skip: float32 [128], replicated, may hold values from -4 to 4
Outputs:
- gated: bfloat16 [1024, 1024, 128], P('row', 'col')
All inputs are finite; a program needn't handle non-finite values.
Results may differ from a plain program's by a relative error of at most 0.001.
Values may be sent and summed in bfloat16 or wider, within the bound.
A program may use at most 192 MiB of HBM per device.

v0:
```python
import math

import jax
import jax.numpy as jnp
from jax import lax
from jax.sharding import PartitionSpec as P

highest = lax.Precision.HIGHEST
full_turn = 2.0 * math.pi


def unit_roots(row_len, col_len, period, sign_value):
    left_iota = lax.broadcasted_iota(jnp.int32, (row_len, col_len), 0)
    right_iota = lax.broadcasted_iota(jnp.int32, (row_len, col_len), 1)
    phases = left_iota * right_iota % period
    angles = phases.astype(jnp.float32) * (sign_value * full_turn / period)
    return (jnp.cos(angles), jnp.sin(angles))


def rotation(row_len, col_len, period, sign_value):
    cosine, sine_part = unit_roots(row_len, col_len, period, sign_value)
    return jnp.stack([jnp.stack([cosine, -sine_part]), jnp.stack([sine_part, cosine])])


def rotate(complex_pair, cosine, sine_part):
    return jnp.stack(
        [
            complex_pair[0] * cosine - complex_pair[1] * sine_part,
            complex_pair[0] * sine_part + complex_pair[1] * cosine,
        ]
    )


def convolve(value, gate, filter_real, filter_imag, skip):
    row_count = lax.axis_size("row")
    col_count = lax.axis_size("col")
    local_rows, local_cols, channels = value.shape
    grid_rows = local_rows * row_count
    grid_cols = local_cols * col_count
    narrow = local_cols // row_count
    local_freq = grid_rows // (row_count * col_count)
    inner_len = min(128, grid_rows)
    outer_len = grid_rows // inner_len
    period = grid_rows * grid_cols
    pieces = value.reshape(local_rows, row_count, narrow, channels)
    columns = lax.all_to_all(pieces, "row", split_axis=1, concat_axis=0, tiled=True)
    real_part = columns.reshape(outer_len, inner_len, narrow, channels).astype(jnp.float32)
    first_matrix = rotation(outer_len, outer_len, outer_len, -1.0)[:, 0]
    interim = jnp.einsum("oku,uwjc->okwjc", first_matrix, real_part, precision=highest)
    row_cos, row_sin = unit_roots(outer_len, inner_len, grid_rows, -1.0)
    interim = rotate(interim, row_cos[:, :, None, None], row_sin[:, :, None, None])
    second_matrix = rotation(inner_len, inner_len, inner_len, -1.0)
    spectrum = jnp.einsum("oibw,ikwjc->obkjc", second_matrix, interim, precision=highest)
    spectrum = spectrum.reshape(2, grid_rows, narrow, channels)
    row_index = lax.axis_index("row")
    col_index = lax.axis_index("col")
    frequency = lax.broadcasted_iota(jnp.int32, (grid_rows, narrow), 0)
    position = (
        col_index * local_cols
        + row_index * narrow
        + lax.broadcasted_iota(jnp.int32, (grid_rows, narrow), 1)
    )
    phases = frequency * position % period
    angles = phases.astype(jnp.float32) * (-full_turn / period)
    twist_cos = jnp.cos(angles)[:, :, None]
    twist_sin = jnp.sin(angles)[:, :, None]
    spectrum = rotate(spectrum, twist_cos, twist_sin)
    arrived = lax.all_to_all(
        spectrum.reshape(2, grid_rows, 1, narrow, channels),
        ("row", "col"),
        split_axis=1,
        concat_axis=2,
        tiled=True,
    )
    arrived = arrived.reshape(2, local_freq, row_count, col_count, narrow, channels)
    col_matrix = rotation(col_count, col_count, col_count, -1.0)
    interim = jnp.einsum("oiac,iprcjz->oprajz", col_matrix, arrived, precision=highest)
    col_cos, col_sin = unit_roots(col_count, local_cols, grid_cols, -1.0)
    col_cos = jnp.transpose(col_cos.reshape(col_count, row_count, narrow), (1, 0, 2))
    col_sin = jnp.transpose(col_sin.reshape(col_count, row_count, narrow), (1, 0, 2))
    interim = rotate(interim, col_cos[None, :, :, :, None], col_sin[None, :, :, :, None])
    wide_matrix = rotation(local_cols, local_cols, local_cols, -1.0).reshape(
        2, 2, local_cols, row_count, narrow
    )
    frequencies = jnp.einsum("oibrj,iprajz->obapz", wide_matrix, interim, precision=highest)
    frequencies = frequencies.reshape(2, grid_cols, local_freq, channels)
    filtered = jnp.stack(
        [
            frequencies[0] * filter_real - frequencies[1] * filter_imag,
            frequencies[0] * filter_imag + frequencies[1] * filter_real,
        ]
    )
    filtered = filtered.reshape(2, local_cols, col_count, local_freq, channels)
    back_wide = rotation(local_cols, local_cols, local_cols, 1.0).reshape(
        2, 2, row_count, narrow, local_cols
    )
    interim = jnp.einsum("oirjb,ibapz->orjapz", back_wide, filtered, precision=highest)
    back_cos, back_sin = unit_roots(local_cols, col_count, grid_cols, 1.0)
    back_cos = back_cos.reshape(row_count, narrow, col_count)
    back_sin = back_sin.reshape(row_count, narrow, col_count)
    interim = rotate(interim, back_cos[:, :, :, None, None], back_sin[:, :, :, None, None])
    back_cols = rotation(col_count, col_count, col_count, 1.0)
    leaving = jnp.einsum("oica,irjapz->oprcjz", back_cols, interim, precision=highest)
    returned = lax.all_to_all(
        leaving.reshape(2, 1, local_freq, row_count * col_count, narrow, channels),
        ("row", "col"),
        split_axis=3,
        concat_axis=1,
        tiled=True,
    )
    returned = returned.reshape(2, grid_rows, narrow, channels)
    returned = rotate(returned, twist_cos, -twist_sin)
    returned = returned.reshape(2, inner_len, outer_len, narrow, channels)
    back_inner = rotation(inner_len, inner_len, inner_len, 1.0)
    interim = jnp.einsum("oinb,ibajz->onajz", back_inner, returned, precision=highest)
    inner_cos, inner_sin = unit_roots(inner_len, outer_len, grid_rows, 1.0)
    interim = rotate(interim, inner_cos[:, :, None, None], inner_sin[:, :, None, None])
    back_outer = rotation(outer_len, outer_len, outer_len, 1.0)[0]
    convolved = jnp.einsum("ima,inajz->mnjz", back_outer, interim, precision=highest)
    convolved = convolved.reshape(grid_rows, 1, narrow, channels) * (1.0 / period)
    settled = lax.all_to_all(convolved, "row", split_axis=0, concat_axis=1, tiled=True)
    settled = settled.reshape(local_rows, local_cols, channels)
    result = gate.astype(jnp.float32) * (settled + skip * value.astype(jnp.float32))
    return result.astype(jnp.bfloat16)


def shards(value, gate, filter_real, filter_imag, skip):
    return convolve(value, gate, filter_real, filter_imag, skip)


def solution(mesh):
    return jax.shard_map(
        shards,
        mesh=mesh,
        in_specs=(
            P("row", "col", None),
            P("row", "col", None),
            P(None, ("row", "col"), None),
            P(None, ("row", "col"), None),
            P(),
        ),
        out_specs=P("row", "col", None),
        check_vma=False,
    )
```

profile of v0, /device:TPU:0, one launch (start us, length us, event | category | flops | bytes accessed | tf_op | source)
XLA Modules:
  0.0 2618.0 jit_solution(3476466117330615844)
XLA Ops:
  0.0 8.4 copy.104
  8.4 5.6 all-to-all-start
  14.0 0.1 fusion.136
  14.1 0.1 copy.106
  14.2 0.1 copy.107
  14.4 0.1 fusion.138
  14.5 0.3 fusion.96
  14.8 0.3 multiply_sine_fusion
  15.1 2.1 fusion.61
  17.2 90.7 %all-to-all-done = bf16[256,4,32,128]{3,2,0,1:T(8,128)(2,1)} async-done(((bf16[256,4,32,128]{3,2,0,1:T(8,128)(2,1)}), bf16[256,4,32,128]{3,2,0,1:T(8,128)(2,1)}, u32[]{:S(2)}, u32[]{:S(2)}) %all-to-all-start) | async-done | bytes 8388640 | tf_op jit(solution)/shard_map/all_to_all | solution.py:46
  107.9 27.7 %fusion.35 = f32[2,8,128,32,128]{4,1,3,2,0:T(8,128)} fusion(bf16[8,128,32,128]{3,2,1,0:T(8,128)(2,1)} %bitcast.20, f32[1,2,8,8]{3,2,1,0:T(8,128)S(1)} %get-tuple-element.34, f32[1,2,8,8]{3,2,1,0:T(8,128)S(1)} %get-tuple-element.33), kind=kOutput, calls=%fused_computation.51 | convolution fusion | flops 805306496 | bytes 41944064 | tf_op jit(solution)/shard_map/oku,uwjc->okwjc/dot_general | solution.py:49
  135.6 22.2 multiply_subtract_fusion.5
  157.8 12.6 pad_maximum_fusion
  170.4 45.7 %fusion.17 = f32[2,128,8,32,128]{4,1,3,2,0:T(8,128)} fusion(f32[2,8,128,32,128]{4,1,3,2,0:T(8,128)S(1)} %pad_maximum_fusion, f32[1,2,128,128]{3,2,1,0:T(8,128)S(1)} %get-tuple-element.28, f32[1,2,128,128]{3,2,1,0:T(8,128)S(1)} %get-tuple-element.27), kind=kOutput, calls=%fused_computation.25 | convolution fusion | flops 25769869312 | bytes 67371008 | tf_op jit(solution)/shard_map/oibw,ikwjc->obkjc/dot_general | solution.py:53
  216.1 21.2 fusion.149
  237.3 15.4 copy.109
  252.7 19.8 copy.110
  272.5 17.4 multiply_subtract_fusion.4
  289.9 12.7 maximum_bitcast_fusion
  302.5 13.6 copy.111
  316.1 5.6 all-to-all-start.1
  321.8 0.1 fusion.137
  321.8 0.1 multiply_sine_fusion.3
  321.9 0.5 copy-done.10
  322.4 0.1 copy-done.12
  322.5 0.6 fusion.115
  323.1 0.3 fusion.98
  323.5 0.7 fusion.114
  324.2 0.3 fusion.92
  324.5 1.0 fusion.97
  325.5 720.4 %all-to-all-done.1 = f32[2,1024,1,32,128]{4,3,0,2,1:T(8,128)} async-done(((f32[2,1024,1,32,128]{4,3,0,2,1:T(8,128)}), f32[2,1024,1,32,128]{4,3,0,2,1:T(8,128)}, u32[]{:S(2)}, u32[]{:S(2)}) %all-to-all-start.1) | async-done | bytes 33554464 | tf_op jit(solution)/shard_map/all_to_all | solution.py:68
  1046.0 12.8 copy.112
  1058.8 44.0 %fusion.30 = f32[2,32,4,8,32,128]{5,3,0,4,2,1:T(8,128)} fusion(f32[2,32,4,8,32,128,1]{5,4,1,3,2,0,6:T(8,128)S(1)} %bitcast.189, f32[1,2,8,8]{3,2,1,0:T(8,128)S(1)} %copy-done.5, f32[1,2,8,8]{3,2,1,0:T(8,128)S(1)} %copy-done.7), kind=kOutput, calls=%fused_computation.50 | convolution fusion | flops 1610612992 | bytes 67109888 | tf_op jit(solution)/shard_map/oiac,iprcjz->oprajz/dot_general | solution.py:77
  1102.9 17.1 multiply_subtract_fusion.3
  1120.0 18.5 maximum_bitcast_fusion.1
  1138.4 50.4 %fusion.27 = f32[2,128,8,32,128]{4,1,0,2,3:T(8,128)} fusion(f32[2,32,4,8,32,128,1]{5,3,0,4,2,1,6:T(8,128)} %maximum_bitcast_fusion.1, f32[2,2,128,4,32,1,1]{2,4,3,1,0,6,5:T(8,128)S(1)} %maximum_bitcast_fusion.46), kind=kOutput, calls=%fused_computation.49 | convolution fusion | flops 25769803776 | bytes 67371008 | tf_op jit(solution)/shard_map/oibrj,iprajz->obapz/dot_general | solution.py:85
  1188.8 17.8 fusion.148
  1206.6 17.9 copy.116
  1224.5 19.6 copy.117
  1244.1 34.4 %fusion.22 = (f32[1024,32,128]{2,1,0:T(8,128)}, f32[1024,32,128]{2,1,0:T(8,128)}) fusion(f32[1024,32,128]{2,1,0:T(8,128)} %param.8, f32[1,128,8,32,128]{4,3,2,1,0:T(8,128)} %copy.117, f32[1024,32,128]{2,1,0:T(8,128)} %param.7, f32[1,128,8,32,128]{4,3,2,1,0:T(8,128)} %copy.116), kind=kLoop, calls=%fused_computation.31 | loop fusion | flops 25165824 | bytes 100663296 | tf_op jit(solution)/shard_map/sub | solution.py:89
  1278.5 15.6 copy.118
  1294.2 15.3 copy.119
  1309.5 35.3 %fusion.21 = f32[2,4,32,8,32,128]{5,2,4,3,1,0:T(8,128)} fusion(f32[1,128,8,32,128]{4,1,0,3,2:T(8,128)S(1)} %copy.119, f32[1,128,8,32,128]{4,1,0,3,2:T(8,128)S(1)} %copy.118, f32[1,1,4,32,128]{4,3,1,2,0:T(8,128)S(1)} %copy-done.3, f32[1,1,4,32,128]{4,3,1,2,0:T(8,128)S(1)} %copy-done.2, f32[1,1,4,32,128]{4,3,1,2,0:T(8,128)S(1)} %copy-done.1), kind=kOutput, calls=%fused_computation.27 | convolution fusion | flops 25778388992 | bytes 67305472 | tf_op jit(solution)/shard_map/oirjb,ibapz->orjapz/dot_general | solution.py:97
  1344.8 21.5 multiply_subtract_fusion.2
  1366.3 12.9 maximum_bitcast_fusion.4
  1379.2 60.4 %fusion.24 = f32[2,32,4,8,32,128]{5,3,0,1,4,2:T(8,128)} fusion(f32[2,4,32,8,32,128,1]{5,2,4,3,1,0,6:T(8,128)S(1)} %maximum_bitcast_fusion.4, f32[1,2,8,8]{3,2,1,0:T(8,128)S(1)} %copy-done.15, f32[1,2,8,8]{3,2,1,0:T(8,128)S(1)} %copy-done.14), kind=kOutput, calls=%fused_computation.48 | convolution fusion | flops 1610612992 | bytes 67109888 | tf_op jit(solution)/shard_map/oica,irjapz->oprcjz/dot_general | solution.py:103
  1439.5 28.3 %copy.121 = f32[2,32,4,8,32,128]{5,4,3,2,1,0:T(8,128)S(1)} copy(f32[2,32,4,8,32,128]{5,3,0,1,4,2:T(8,128)} %fusion.24) | data formatting | bytes 67108864 | tf_op jit(solution)/shard_map/oica,irjapz->oprcjz/transpose | solution.py:103
  1467.8 13.5 copy.122
  1481.3 4.8 all-to-all-start.2
  1486.2 0.3 fusion.95
  1486.5 0.3 multiply_sine_fusion.1
  1486.8 0.6 fusion.76
  1487.4 722.9 %all-to-all-done.2 = f32[2,1,32,32,32,128]{5,4,2,0,1,3:T(8,128)} async-done(((f32[2,1,32,32,32,128]{5,4,2,0,1,3:T(8,128)}), f32[2,1,32,32,32,128]{5,4,2,0,1,3:T(8,128)}, u32[]{:S(2)}, u32[]{:S(2)}) %all-to-all-start.2) | async-done | bytes 33554464 | tf_op jit(solution)/shard_map/all_to_all | solution.py:104
  2210.4 23.0 copy.194
  2233.3 21.3 fusion.147
  2254.6 23.1 multiply_subtract_fusion.1
  2277.7 36.5 %fusion.20 = f32[2,128,8,32,128]{4,1,3,2,0:T(8,128)} fusion(f32[1,128,8,32,128]{4,1,0,3,2:T(8,128)} %get-tuple-element.10, f32[1,128,8,32,128]{4,1,0,3,2:T(8,128)} %get-tuple-element.9, f32[1,2,128,128]{3,2,1,0:T(8,128)S(1)} %get-tuple-element.26, f32[1,2,128,128]{3,2,1,0:T(8,128)S(1)} %get-tuple-element.25), kind=kOutput, calls=%fused_computation.26 | convolution fusion | flops 25778257920 | bytes 67371008 | tf_op jit(solution)/shard_map/oinb,ibajz->onajz/dot_general | solution.py:115
  2314.3 17.3 multiply_subtract_fusion
  2331.6 18.4 pad_maximum_fusion.1
  2350.0 54.7 %bitcast_multiply_fusion = f32[8,128,32,128]{3,0,2,1:T(8,128)S(1)} fusion(f32[2,128,8,32,128]{4,1,3,2,0:T(8,128)} %pad_maximum_fusion.1, f32[1,8,8]{2,1,0:T(8,128)S(1)} %copy-done.11, f32[1,8,8]{2,1,0:T(8,128)S(1)} %copy-done.13), kind=kOutput, calls=%fused_computation.28 | convolution fusion | flops 809500800 | bytes 50332160 | tf_op jit(solution)/shard_map/ima,inajz->mnjz/dot_general | solution.py:119
  2404.7 5.3 copy.129
  2410.0 185.9 %all_to_all.60 = f32[1024,1,32,128]{3,2,1,0:T(8,128)S(1)} all-to-all(f32[1024,1,32,128]{3,2,1,0:T(8,128)S(1)} %bitcast.192), channel_id=1, replica_groups=mesh['row'=4,'col'=8] {'row'}, dimensions={0} | all-to-all | bytes 33554432 | tf_op jit(solution)/shard_map/all_to_all | solution.py:121
  2595.9 7.0 copy.131
  2602.9 14.9 multiply_convert_fusion
  (46 shorter events, 0.3 us)
Async XLA Ops:
  8.4 99.5 %all-to-all-start = ((bf16[256,4,32,128]{3,2,0,1:T(8,128)(2,1)}), bf16[256,4,32,128]{3,2,0,1:T(8,128)(2,1)}, u32[]{:S(2)}, u32[]{:S(2)}) async-start(bf16[256,4,32,128]{3,2,0,1:T(8,128)(2,1)} %copy.104), calls=%async_computation | async-start | bytes 16777216 | tf_op jit(solution)/shard_map/all_to_all | solution.py:46
  14.4 121.2 %copy-start.16 = (s32[32]{0:T(128)}, s32[32]{0:T(128)S(1)}, u32[]{:S(2)}) copy-start(s32[32]{0:T(128)S(1)} %iota_add_fusion) | copy-start | bytes 388
  14.5 121.1 %copy-start.4 = (f32[1,2,8,8]{3,2,1,0:T(8,128)}, f32[1,2,8,8]{3,2,1,0:T(8,128)S(1)}, u32[]{:S(2)}) copy-start(f32[1,2,8,8]{3,2,1,0:T(8,128)S(1)} %get-tuple-element.33) | copy-start | bytes 1540
  14.5 121.1 %copy-start.6 = (f32[1,2,8,8]{3,2,1,0:T(8,128)}, f32[1,2,8,8]{3,2,1,0:T(8,128)S(1)}, u32[]{:S(2)}) copy-start(f32[1,2,8,8]{3,2,1,0:T(8,128)S(1)} %get-tuple-element.34) | copy-start | bytes 1540
  237.3 15.4 copy-start
  316.1 729.8 %all-to-all-start.1 = ((f32[2,1024,1,32,128]{4,3,0,2,1:T(8,128)}), f32[2,1024,1,32,128]{4,3,0,2,1:T(8,128)}, u32[]{:S(2)}, u32[]{:S(2)}) async-start(f32[2,1024,1,32,128]{4,3,0,2,1:T(8,128)} %copy.111), calls=%async_computation.1 | async-start | bytes 67108864 | tf_op jit(solution)/shard_map/all_to_all | solution.py:68
  321.8 0.6 copy-start.10
  321.9 0.6 copy-start.12
  325.5 733.3 %copy-start.5 = (f32[1,2,8,8]{3,2,1,0:T(8,128)S(1)}, f32[1,2,8,8]{3,2,1,0:T(8,128)}, u32[]{:S(2)}) copy-start(f32[1,2,8,8]{3,2,1,0:T(8,128)} %copy-done.4) | copy-start | bytes 1540
  325.5 733.3 %copy-start.7 = (f32[1,2,8,8]{3,2,1,0:T(8,128)S(1)}, f32[1,2,8,8]{3,2,1,0:T(8,128)}, u32[]{:S(2)}) copy-start(f32[1,2,8,8]{3,2,1,0:T(8,128)} %copy-done.6) | copy-start | bytes 1540
  1294.1 15.3 copy-start.1
  1294.1 15.3 copy-start.2
  1294.2 15.3 copy-start.3
  1309.5 35.3 %copy-start.8 = (f32[4,32,8]{1,2,0:T(8,128)S(1)}, f32[4,32,8]{1,2,0:T(8,128)}, u32[]{:S(2)}) copy-start(f32[4,32,8]{1,2,0:T(8,128)} %get-tuple-element.35) | copy-start | bytes 12292
  1309.5 35.3 %copy-start.9 = (f32[4,32,8]{1,2,0:T(8,128)S(1)}, f32[4,32,8]{1,2,0:T(8,128)}, u32[]{:S(2)}) copy-start(f32[4,32,8]{1,2,0:T(8,128)} %get-tuple-element.36) | copy-start | bytes 12292
  1366.3 12.9 copy-start.14
  1366.3 12.9 copy-start.15
  1481.3 5.5 copy-start.17
  1481.3 729.0 %all-to-all-start.2 = ((f32[2,1,32,32,32,128]{5,4,2,0,1,3:T(8,128)}), f32[2,1,32,32,32,128]{5,4,2,0,1,3:T(8,128)}, u32[]{:S(2)}, u32[]{:S(2)}) async-start(f32[2,1,32,32,32,128]{5,4,2,0,1,3:T(8,128)} %copy.122), calls=%async_computation.2 | async-start | bytes 67108864 | tf_op jit(solution)/shard_map/all_to_all | solution.py:104
  2331.6 18.4 copy-start.11
  2331.6 18.4 copy-start.13
  2595.9 7.0 copy-start.18
where the time goes:
time: 2630 us; the launch traced here: 2620 us
  waiting for transfers between devices  1530 us (58%)
  matrix products  355 us (13%)
  local copies, waits for them, and re-layouts  277 us (11%)
  other arithmetic  250 us (10%)
  blocking collectives  186 us (7%)
    all_to_all x1, waiting for transfers between devices, convolve(): lax.all_to_all(leaving.reshape(2, 1, local_freq, row_count * col_count, n...  723 us
    all_to_all x1, waiting for transfers between devices, convolve(): lax.all_to_all(spectrum.reshape(2, grid_rows, 1, narrow, channels), ('row...  720 us
    all_to_all x1, blocking collectives, convolve(): lax.all_to_all(convolved, 'row', split_axis=0, concat_axis=1, tiled=True)  186 us
    sub x6, other arithmetic, rotate(): complex_pair[0] * cosine - complex_pair[1] * sine_part  119 us
    all_to_all x1, waiting for transfers between devices, convolve(): lax.all_to_all(pieces, 'row', split_axis=1, concat_axis=0, tiled=True)  90.7 us
    another operation x4, other arithmetic, rotate(): jnp.stack([complex_pair[0] * cosine - complex_pair[1] * sine_part, comple...  62.4 us
    dot_general x1, matrix products, convolve(): jnp.einsum('oica,irjapz->oprcjz', back_cols, interim, precision=highest)  60.4 us
    slice x3, local copies, waits for them, and re-layouts, rotate(): complex_pair[0] * cosine - complex_pair[1] * sine_part  57.9 us
  transfers between devices with their start and end apart: 3, of which 3 were waited for; matrix products, arithmetic and copies ran while one was open for 0% of the time, Pallas kernels for 0%

commit v1 on v0

v1 whole, which is shorter than its diff:
```python
import math

import jax
import jax.numpy as jnp
from jax import lax
from jax.sharding import PartitionSpec as P

full_turn = 2.0 * math.pi
code_top = 250.0
chunk_count = 2


def phase_table(left, right, period):
    angles = (left * right % period).astype(jnp.float32) * (full_turn / period)
    return jnp.cos(angles), jnp.sin(angles)


def contract(spec, left, right):
    return jnp.einsum(
        spec, left, right, precision=lax.Precision.HIGH, preferred_element_type=jnp.float32
    )


def encode(array, largest):
    scaled = array * (code_top / largest)
    return (scaled * jnp.abs(scaled)).astype(jnp.float16)


def decode(coded, largest):
    wide = coded.astype(jnp.float32)
    root = jnp.sqrt(jnp.abs(wide)) * (largest * (1.0 / code_top))
    return jnp.where(wide < 0.0, -root, root)


def bound_of(array):
    return jnp.maximum(jnp.max(jnp.abs(array)).astype(jnp.float32), 1e-30)


def convolve(value, gate, filter_real, filter_imag, skip):
    row_count = lax.axis_size("row")
    col_count = lax.axis_size("col")
    both = ("row", "col")
    local_rows, local_cols, channels = value.shape
    grid_rows = local_rows * row_count
    grid_cols = local_cols * col_count
    narrow = local_cols // row_count
    devices = row_count * col_count
    local_freq = grid_rows // devices
    period = grid_rows * grid_cols
    width = narrow // chunk_count
    row_index = lax.axis_index("row")
    col_index = lax.axis_index("col")

    freq = jnp.arange(grid_rows, dtype=jnp.int32)
    cosine, sine = phase_table(freq[:, None], freq[None, :], grid_rows)
    col_matrix = jnp.stack(
        [
            cosine.reshape(devices, local_freq, grid_rows),
            -sine.reshape(devices, local_freq, grid_rows),
        ],
        axis=1,
    )

    pieces = value.reshape(local_rows, row_count, chunk_count, width, channels)
    columns = []
    for chunk in range(chunk_count):
        part = lax.all_to_all(
            pieces[:, :, chunk], "row", split_axis=1, concat_axis=0, tiled=True
        )
        columns.append(part.reshape(grid_rows, width, channels))

    kq = jnp.arange(grid_cols, dtype=jnp.int32)

    def row_matrix(chunk):
        source = jnp.arange(devices, dtype=jnp.int32)
        base = source % col_count * local_cols + source // col_count * narrow + chunk * width
        position = base[:, None] + jnp.arange(width, dtype=jnp.int32)[None, :]
        c, s = phase_table(kq[:, None, None], position[None], grid_cols)
        return jnp.stack([jnp.stack([c, s], axis=2), jnp.stack([-s, c], axis=2)])

    twists = []
    for chunk in range(chunk_count):
        position = (
            col_index * local_cols
            + row_index * narrow
            + chunk * width
            + jnp.arange(width, dtype=jnp.int32)
        )
        c, s = phase_table(freq[:, None], position[None, :], period)
        c = c.reshape(devices, local_freq, width).transpose(0, 2, 1)[..., None]
        s = s.reshape(devices, local_freq, width).transpose(0, 2, 1)[..., None]
        twists.append((c, s))

    row_parts = [row_matrix(chunk) for chunk in range(chunk_count)]
    frequencies = None
    for chunk in range(chunk_count):
        spectrum = contract("diap,pwz->diwaz", col_matrix, columns[chunk].astype(jnp.float32))
        c, s = twists[chunk]
        real, imag = spectrum[:, 0], spectrum[:, 1]
        spectrum = jnp.stack([real * c + imag * s, imag * c - real * s], axis=1)
        largest = bound_of(columns[chunk]) * float(grid_rows)
        every = lax.all_gather(largest, both)
        arrived = lax.all_to_all(encode(spectrum, largest), both, 0, 0, tiled=True)
        arrived = decode(arrived, every[:, None, None, None, None])
        term = contract("oksiw,siwaz->okaz", row_parts[chunk], arrived)
        frequencies = term if frequencies is None else frequencies + term

    real, imag = frequencies[0], frequencies[1]
    filtered = jnp.stack(
        [
            real * filter_real - imag * filter_imag,
            real * filter_imag + imag * filter_real,
        ]
    )

    settled = []
    for chunk in range(chunk_count):
        leaving = contract("oksiw,okaz->siwaz", row_parts[chunk], filtered)
        largest = bound_of(leaving)
        every = lax.all_gather(largest, both)
        returned = lax.all_to_all(encode(leaving, largest), both, 0, 0, tiled=True)
        returned = decode(returned, every[:, None, None, None, None] * (1.0 / period))
        c, s = twists[chunk]
        real, imag = returned[:, 0], returned[:, 1]
        returned = jnp.stack([real * c - imag * s, imag * c + real * s], axis=1)
        convolved = contract("diap,diwaz->pwz", col_matrix, returned)
        largest = bound_of(convolved)
        every = lax.all_gather(largest, "row")
        coded = encode(convolved, largest).reshape(row_count, local_rows, width, channels)
        coded = lax.all_to_all(coded, "row", 0, 0, tiled=True)
        settled.append(decode(coded, every[:, None, None, None]))
    settled = jnp.stack(settled, axis=1)
    settled = settled.transpose(2, 0, 1, 3, 4).reshape(local_rows, local_cols, channels)
    result = gate.astype(jnp.float32) * (settled + skip * value.astype(jnp.float32))
    return result.astype(jnp.bfloat16)


def solution(mesh):
    return jax.shard_map(
        convolve,
        mesh=mesh,
        in_specs=(
            P("row", "col", None),
            P("row", "col", None),
            P(None, ("row", "col"), None),
            P(None, ("row", "col"), None),
            P(),
        ),
        out_specs=P("row", "col", None),
        check_vma=False,
    )
```

time: 2630 us -> 1400 us (0.53)
  waiting for transfers between devices: 1530 us -> 219 us
  local copies, waits for them, and re-layouts: 277 us -> 36.4 us
  blocking collectives: 186 us -> 417 us
  matrix products: 355 us -> 396 us
  other arithmetic: 250 us -> 284 us
    all_to_all x3 -> x8, waiting for transfers between devices: 1530 us -> 219 us  [the longest x2 102 us: convolve(): arrived = lax.all_to_all(encode(spectrum, largest), both, 0, 0, tiled=True)]
    unnamed x0 -> x3, blocking collectives: none -> 417 us
    all_to_all x1 -> x0, blocking collectives: 186 us -> none  [convolve(): lax.all_to_all(convolved, 'row', split_axis=0, concat_axis=1, tiled=True)]
    slice x7 -> x0, local copies, waits for them, and re-layouts: 133 us -> none  [the longest x3 57.9 us: rotate(): complex_pair[0] * cosine - complex_pair[1] * sine_part]
    sub x7 -> x1, other arithmetic: 153 us -> 20.2 us  [convolve(): returned = jnp.stack([real * c - imag * s, imag * c + real * s], axis=1)]
    select_n x0 -> x4, other arithmetic: none -> 64.9 us  [decode(): return jnp.where(wide < 0.0, -root, root)]
    convert_element_type x0 -> x6, other arithmetic: none -> 46.8 us  [encode(): return (scaled * jnp.abs(scaled)).astype(jnp.float16)]
    dot_general x8, matrix products: 355 us -> 396 us  [contract(): jnp.einsum(spec, left, right, precision=lax.Precision.HIGH, preferred_ele...]
  transfers between devices with their start and end apart: 3 -> 8, of which waited for: 3 -> 5; matrix products, arithmetic and copies ran while one was open for 0% -> 28% of each run, Pallas kernels for 0% -> 0%
where the time goes in v1:
time: 1400 us; the launch traced here: 1390 us
  blocking collectives  417 us (30%)
  matrix products  396 us (28%)
  other arithmetic  284 us (20%)
  waiting for transfers between devices  219 us (16%)
  starting transfers between devices  37.4 us (3%)
  local copies, waits for them, and re-layouts  36.4 us (3%)
    unnamed x3, blocking collectives  417 us
    dot_general x8, matrix products, contract(): jnp.einsum(spec, left, right, precision=lax.Precision.HIGH, preferred_ele...  396 us
    all_to_all x2, waiting for transfers between devices, convolve(): arrived = lax.all_to_all(encode(spectrum, largest), both, 0, 0, tiled=True)  102 us
    all_to_all x2, waiting for transfers between devices, convolve(): returned = lax.all_to_all(encode(leaving, largest), both, 0, 0, tiled=True)  85.8 us
    select_n x4, other arithmetic, decode(): return jnp.where(wide < 0.0, -root, root)  64.9 us
    convert_element_type x6, other arithmetic, encode(): return (scaled * jnp.abs(scaled)).astype(jnp.float16)  46.8 us
    another operation x1, other arithmetic, convolve(): jnp.stack([real * filter_real - imag * filter_imag, real * filter_imag +...  34 us
    another operation x3, other arithmetic, convolve(): settled = jnp.stack(settled, axis=1)  28.5 us
  transfers between devices with their start and end apart: 8, of which 5 were waited for; matrix products, arithmetic and copies ran while one was open for 28% of the time, Pallas kernels for 0%

profile of v1, /device:TPU:0, one launch (start us, length us, event | category | flops | bytes accessed | tf_op | source)
XLA Modules:
  0.0 1394.3 jit_solution(10236008082658331679)
XLA Ops:
  0.0 5.8 slice_bitcast_fusion.2
  5.8 4.7 copy.45
  10.5 5.2 all-to-all-start
  15.7 6.8 copy.48
  22.5 2.1 fusion.89
  24.7 18.9 %fusion.73 = (f32[32,1,32,1024]{3,2,1,0:T(8,128)}, f32[32,1,32,1024]{3,2,1,0:T(8,128)}) fusion(s32[32,32]{1,0:T(8,128)S(1)} %multiply_add_fusion.4), kind=kLoop, calls=%fused_computation.142 | loop fusion | flops 15728640 | bytes 8392704 | tf_op jit(solution)/shard_map/cos | solution.py:15
  43.6 20.6 %all-to-all-done = bf16[256,4,16,128]{3,0,2,1:T(8,128)(2,1)} async-done(((bf16[256,4,16,128]{3,0,2,1:T(8,128)(2,1)}), bf16[256,4,16,128]{3,0,2,1:T(8,128)(2,1)}, u32[]{:S(2)}, u32[]{:S(2)}) %all-to-all-start) | async-done | bytes 4194336 | tf_op jit(solution)/shard_map/all_to_all | solution.py:67
  64.2 5.1 all-to-all-start.2
  69.3 4.7 copy.46
  74.0 3.4 abs_reduce_fusion.3
  78.1 22.1 %convolution_bitcast_fusion.1 = f32[32,2,16,32,128]{4,3,2,1,0:T(8,128)S(1)} fusion(bf16[1024,16,128,1,1]{2,0,1,4,3:T(8,128)(2,1)} %bitcast.174, f32[32,1,32,1024]{3,2,1,0:T(8,128)} %get-tuple-element.34, f32[32,1,32,1024]{3,2,1,0:T(8,128)} %get-tuple-element.33), kind=kOutput, calls=%fused_computation.72 | convolution fusion | flops 25771900928 | bytes 29360128 | tf_op jit(solution)/shard_map/diap,pwz->diwaz/dot_general | solution.py:19
  100.2 5.6 multiply_add_fusion.3
  105.9 4.8 fusion.12
  110.6 5.8 all-to-all-done.2
  116.4 5.4 all-to-all-start.1
  121.9 8.4 fusion.78
  130.4 1.5 maximum_bitcast_fusion.1
  131.8 4.5 fusion.56
  136.4 1.3 copy-done.2
  137.7 10.5 fusion.76
  148.2 3.4 abs_reduce_fusion.2
  152.4 7.6 maximum_bitcast_fusion.3
  160.0 165.7 %all-reduce.7 = (f32[32]{0:T(128)S(1)}, f32[32]{0:T(128)S(1)}) all-reduce(f32[32]{0:T(128)S(1)} %dynamic-update-slice, f32[32]{0:T(128)S(1)} %dynamic-update-slice.1), channel_id=1, replica_groups=mesh['row'=4,'col'=8] {'row','col'}, use_global_device_ids=true, to_apply=%add | all-reduce | flops 64 | bytes 512
  325.8 2.6 copy.49
  329.2 1.3 copy-done.4
  330.5 18.0 %convolution_bitcast_fusion = f32[32,2,16,32,128]{4,3,2,1,0:T(8,128)S(1)} fusion(bf16[1024,16,128,1,1]{2,0,1,4,3:T(8,128)(2,1)S(1)} %bitcast.175, f32[32,1,32,1024]{3,2,1,0:T(8,128)S(1)} %copy-done.4, f32[32,1,32,1024]{3,2,1,0:T(8,128)S(1)} %copy-done.3), kind=kOutput, calls=%fused_computation.71 | convolution fusion | flops 25771900928 | bytes 29360128 | tf_op jit(solution)/shard_map/diap,pwz->diwaz/dot_general | solution.py:19
  348.5 5.6 multiply_add_fusion.2
  354.1 4.8 fusion.13
  358.9 4.5 all-to-all-start.3
  363.5 16.3 %negate_select_fusion.3 = f32[32,2,16,32,128]{4,3,2,1,0:T(8,128)} fusion(f16[32,2,16,32,128]{4,3,2,1,0:T(8,128)(2,1)} %all-to-all-done.1, f32[32]{0:T(128)S(1)} %broadcast_multiply_fusion.5), kind=kLoop, calls=%fused_computation.12 | loop fusion | flops 25165824 | bytes 25165952 | tf_op jit(solution)/shard_map/jit(_where)/select_n | solution.py:32
  379.8 66.3 %fusion.27 = f32[2,1024,32,128,1,1]{3,1,5,4,2,0:T(8,128)} fusion(f32[32,2,16,32,128]{4,3,2,1,0:T(8,128)} %negate_select_fusion.3, f32[1,1024,32,2,16]{1,2,4,3,0:T(8,128)} %copy-done.2, f32[1,1024,32,2,16]{1,2,4,3,0:T(8,128)S(1)} %copy-done.1), kind=kOutput, calls=%fused_computation.51 | convolution fusion | flops 51541704704 | bytes 58720256 | tf_op jit(solution)/shard_map/oksiw,siwaz->okaz/dot_general | solution.py:19
  446.0 102.3 %all-to-all-done.3 = f16[32,2,16,32,128]{4,3,2,1,0:T(8,128)(2,1)} async-done(((f16[32,2,16,32,128]{4,3,2,1,0:T(8,128)(2,1)}), f16[32,2,16,32,128]{4,3,2,1,0:T(8,128)(2,1)}, u32[]{:S(2)}, u32[]{:S(2)}) %all-to-all-start.3) | async-done | bytes 8388640 | tf_op jit(solution)/shard_map/all_to_all | solution.py:103
  548.4 16.1 %negate_select_fusion.2 = f32[32,2,16,32,128]{4,3,2,1,0:T(8,128)} fusion(f16[32,2,16,32,128]{4,3,2,1,0:T(8,128)(2,1)} %all-to-all-done.3, f32[32]{0:T(128)S(1)} %copy-done.13), kind=kLoop, calls=%fused_computation.10 | loop fusion | flops 25165824 | bytes 25165952 | tf_op jit(solution)/shard_map/jit(_where)/select_n | solution.py:32
  564.5 68.3 %bitcast_add_fusion = f32[2,1024,32,128]{3,1,2,0:T(8,128)} fusion(f32[2,1024,32,128,1,1]{3,1,5,4,2,0:T(8,128)} %fusion.27, f32[32,2,16,32,128]{4,3,2,1,0:T(8,128)} %negate_select_fusion.2, f32[1,1024,32,2,16]{1,2,4,3,0:T(8,128)} %get-tuple-element.24, f32[1,1024,32,2,16]{1,2,4,3,0:T(8,128)} %get-tuple-element.23), kind=kOutput, calls=%fused_computation.1 | convolution fusion | flops 51550093312 | bytes 92274688 | tf_op jit(solution)/shard_map/oksiw,siwaz->okaz/dot_general | solution.py:19
  632.8 34.0 %subtract_bitcast_fusion = (f32[1,1024,32,128]{3,1,2,0:T(8,128)}, f32[1,1024,32,128]{3,1,2,0:T(8,128)}) fusion(f32[2,1024,32,128]{3,1,2,0:T(8,128)} %bitcast_add_fusion, f32[1024,32,128]{2,1,0:T(8,128)} %param.8, f32[1024,32,128]{2,1,0:T(8,128)} %param.7), kind=kLoop, calls=%fused_computation.60 | loop fusion | flops 25165824 | bytes 100663296 | tf_op jit(solution)/shard_map/stack | solution.py:109
  666.8 76.5 %abs_reduce_fusion.1 = (f32[]{:T(128)}, f32[32,2,16,32,128]{4,2,3,1,0:T(8,128)}) fusion(f32[2,1024,32,2,16,1]{1,2,4,3,0,5:T(8,128)} %fusion.56, f32[1,1024,32,128]{3,1,2,0:T(8,128)} %get-tuple-element.12, f32[1,1024,32,128]{3,1,2,0:T(8,128)} %get-tuple-element.11), kind=kOutput, calls=%fused_computation.58 | convolution fusion | flops 51556384768 | bytes 58720260 | tf_op jit(solution)/shard_map/oksiw,okaz->siwaz/dot_general | solution.py:19
  743.9 13.7 fusion.14
  757.6 3.7 all-to-all-start.4
  761.3 8.5 fusion.55
  769.8 76.3 %abs_reduce_fusion = (f32[]{:T(128)}, f32[32,2,16,32,128]{4,2,3,1,0:T(8,128)}) fusion(f32[2,1024,32,2,16,1]{1,2,4,3,0,5:T(8,128)} %fusion.55, f32[1,1024,32,128]{3,1,2,0:T(8,128)} %get-tuple-element.12, f32[1,1024,32,128]{3,1,2,0:T(8,128)} %get-tuple-element.11), kind=kOutput, calls=%fused_computation.57 | convolution fusion | flops 51556384768 | bytes 58720260 | tf_op jit(solution)/shard_map/oksiw,okaz->siwaz/dot_general | solution.py:19
  846.7 13.7 fusion.15
  860.4 85.8 %all-to-all-done.4 = f16[32,2,16,32,128]{4,3,2,1,0:T(8,128)(2,1)} async-done(((f16[32,2,16,32,128]{4,3,2,1,0:T(8,128)(2,1)}), f16[32,2,16,32,128]{4,3,2,1,0:T(8,128)(2,1)}, u32[]{:S(2)}, u32[]{:S(2)}) %all-to-all-start.4) | async-done | bytes 8388640 | tf_op jit(solution)/shard_map/all_to_all | solution.py:121
  946.2 3.7 all-to-all-start.6
  950.1 203.5 %all-reduce.6 = (f32[32]{0:T(128)S(1)}, f32[32]{0:T(128)S(1)}) all-reduce(f32[32]{0:T(128)S(1)} %dynamic-update-slice.4, f32[32]{0:T(128)S(1)} %dynamic-update-slice.2), channel_id=1, replica_groups=mesh['row'=4,'col'=8] {'row','col'}, use_global_device_ids=true, to_apply=%add.4 | all-reduce | flops 64 | bytes 512
  1153.6 16.1 %negate_select_fusion.1 = f32[32,2,16,32,128]{4,3,2,1,0:T(8,128)} fusion(f16[32,2,16,32,128]{4,3,2,1,0:T(8,128)(2,1)} %all-to-all-done.4, f32[32]{0:T(128)S(1)} %broadcast_multiply_fusion.3), kind=kLoop, calls=%fused_computation.8 | loop fusion | flops 25165824 | bytes 25165952 | tf_op jit(solution)/shard_map/jit(_where)/select_n | solution.py:32
  1169.8 16.4 %negate_select_fusion = f32[32,2,16,32,128]{4,3,2,1,0:T(8,128)} fusion(f16[32,2,16,32,128]{4,3,2,1,0:T(8,128)(2,1)} %all-to-all-done.6, f32[32]{0:T(128)S(1)} %broadcast_multiply_fusion.2), kind=kLoop, calls=%fused_computation.6 | loop fusion | flops 25165824 | bytes 25165952 | tf_op jit(solution)/shard_map/jit(_where)/select_n | solution.py:32
  1186.2 20.2 %multiply_subtract_fusion = (f32[32,1,16,32,128]{4,3,2,1,0:T(8,128)}, f32[32,1,16,32,128]{4,3,2,1,0:T(8,128)}, f32[32,1,16,32,128]{4,3,2,1,0:T(8,128)S(1)}, f32[32,1,16,32,128]{4,3,2,1,0:T(8,128)}) fusion(f32[32,2,16,32,128]{4,3,2,1,0:T(8,128)} %negate_select_fusion, f32[32,16,32]{2,1,0:T(8,128)S(1)} %copy-done.8, f32[32,16,32]{2,1,0:T(8,128)S(1)} %copy-done.6, ...), kind=kLoop, calls=%fused_computation.99 | loop fusion | flops 25165824 | bytes 67371008 | tf_op jit(solution)/shard_map/sub | solution.py:125
  1206.4 34.5 %fusion.46 = (f32[]{:T(128)}, f32[1024,16,128,1,1]{2,0,1,4,3:T(8,128)}) fusion(f32[32,1,16,32,128]{4,3,2,1,0:T(8,128)S(1)} %get-tuple-element.49, f32[32,1,16,32,128]{4,3,2,1,0:T(8,128)} %get-tuple-element.50, f32[32,1,32,1024]{3,2,1,0:T(8,128)} %get-tuple-element.34, f32[32,1,32,1024]{3,2,1,0:T(8,128)} %get-tuple-element.33), kind=kOutput, calls=%fused_computation.86 | convolution fusion | flops 25780289536 | bytes 33554436 | tf_op jit(solution)/shard_map/diap,diwaz->pwz/dot_general | solution.py:19
  1241.5 4.9 fusion.41
  1246.4 3.0 copy.59
  1249.5 4.9 all-to-all-start.5
  1254.4 33.8 %fusion.45 = (f32[]{:T(128)}, f32[1024,16,128,1,1]{2,0,1,4,3:T(8,128)}) fusion(f32[32,1,16,32,128]{4,3,2,1,0:T(8,128)} %get-tuple-element.16, f32[32,1,16,32,128]{4,3,2,1,0:T(8,128)} %get-tuple-element.15, f32[32,1,32,1024]{3,2,1,0:T(8,128)} %get-tuple-element.34, f32[32,1,32,1024]{3,2,1,0:T(8,128)} %get-tuple-element.33), kind=kOutput, calls=%fused_computation.83 | convolution fusion | flops 25780289536 | bytes 33554436 | tf_op jit(solution)/shard_map/diap,diwaz->pwz/dot_general | solution.py:19
  1288.9 4.9 fusion.43
  1293.8 3.1 copy.65
  1296.9 4.4 all-to-all-done.5
  1301.3 4.9 all-to-all-start.7
  1306.2 0.7 dynamic-slice
  1306.9 0.8 dynamic-update-slice.3
  1307.6 0.8 dynamic-update-slice.5
  1308.4 47.7 %all-reduce.8 = (f32[4]{0:T(128)S(1)}, f32[4]{0:T(128)S(1)}) all-reduce(f32[4]{0:T(128)S(1)} %dynamic-update-slice.5, f32[4]{0:T(128)S(1)} %dynamic-update-slice.3), channel_id=1, replica_groups=mesh['row'=4,'col'=8] {'row'}, use_global_device_ids=true, to_apply=%add.5 | all-reduce | flops 8 | bytes 64
  1356.1 10.3 fusion.42
  1366.4 10.6 fusion.44
  1377.0 7.6 pad_maximum_fusion
  1384.7 9.2 fusion.25
  (61 shorter events, 1.4 us)
Async XLA Ops:
  10.5 53.7 %all-to-all-start = ((bf16[256,4,16,128]{3,0,2,1:T(8,128)(2,1)}), bf16[256,4,16,128]{3,0,2,1:T(8,128)(2,1)}, u32[]{:S(2)}, u32[]{:S(2)}) async-start(bf16[256,4,16,128]{3,0,2,1:T(8,128)(2,1)} %copy.45), calls=%async_computation | async-start | bytes 8388608 | tf_op jit(solution)/shard_map/all_to_all | solution.py:67
  24.6 75.6 %copy-start.9 = (f32[32,16,32]{2,1,0:T(8,128)}, f32[32,16,32]{2,1,0:T(8,128)S(1)}, u32[]{:S(2)}) copy-start(f32[32,16,32]{2,1,0:T(8,128)S(1)} %get-tuple-element.31) | copy-start | bytes 196612
  24.6 75.6 %copy-start.11 = (f32[32,16,32]{2,1,0:T(8,128)}, f32[32,16,32]{2,1,0:T(8,128)S(1)}, u32[]{:S(2)}) copy-start(f32[32,16,32]{2,1,0:T(8,128)S(1)} %get-tuple-element.32) | copy-start | bytes 196612
  24.6 323.9 %copy-start.5 = (f32[32,16,32]{2,1,0:T(8,128)}, f32[32,16,32]{2,1,0:T(8,128)S(1)}, u32[]{:S(2)}) copy-start(f32[32,16,32]{2,1,0:T(8,128)S(1)} %get-tuple-element.27) | copy-start | bytes 196612
  24.7 323.9 %copy-start.7 = (f32[32,16,32]{2,1,0:T(8,128)}, f32[32,16,32]{2,1,0:T(8,128)S(1)}, u32[]{:S(2)}) copy-start(f32[32,16,32]{2,1,0:T(8,128)S(1)} %get-tuple-element.28) | copy-start | bytes 196612
  64.2 52.2 %all-to-all-start.2 = ((bf16[256,4,16,128]{3,0,2,1:T(8,128)(2,1)}), bf16[256,4,16,128]{3,0,2,1:T(8,128)(2,1)}, u32[]{:S(2)}, u32[]{:S(2)}) async-start(bf16[256,4,16,128]{3,0,2,1:T(8,128)(2,1)} %copy.48), calls=%async_computation.2 | async-start | bytes 8388608 | tf_op jit(solution)/shard_map/all_to_all | solution.py:67
  116.4 242.5 %all-to-all-start.1 = ((f16[32,2,16,32,128]{4,3,2,1,0:T(8,128)(2,1)}), f16[32,2,16,32,128]{4,3,2,1,0:T(8,128)(2,1)}, u32[]{:S(2)}, u32[]{:S(2)}) async-start(f16[32,2,16,32,128]{4,3,2,1,0:T(8,128)(2,1)} %fusion.12), calls=%async_computation.1 | async-start | bytes 16777216 | tf_op jit(solution)/shard_map/all_to_all | solution.py:103
  131.8 4.6 copy-start
  131.8 5.8 copy-start.2
  325.7 3.5 copy-start.3
  325.8 4.7 copy-start.4
  358.9 189.4 %all-to-all-start.3 = ((f16[32,2,16,32,128]{4,3,2,1,0:T(8,128)(2,1)}), f16[32,2,16,32,128]{4,3,2,1,0:T(8,128)(2,1)}, u32[]{:S(2)}, u32[]{:S(2)}) async-start(f16[32,2,16,32,128]{4,3,2,1,0:T(8,128)(2,1)} %fusion.13), calls=%async_computation.3 | async-start | bytes 16777216 | tf_op jit(solution)/shard_map/all_to_all | solution.py:103
  363.5 16.3 %copy-start.1 = (f32[1,1024,32,2,16]{1,2,4,3,0:T(8,128)S(1)}, f32[1,1024,32,2,16]{1,2,4,3,0:T(8,128)}, u32[]{:S(2)}) copy-start(f32[1,1024,32,2,16]{1,2,4,3,0:T(8,128)} %copy-done) | copy-start | bytes 12582916
  379.8 168.6 %copy-start.13 = (f32[32]{0:T(128)S(1)}, f32[32]{0:T(128)}, u32[]{:S(2)}) copy-start(f32[32]{0:T(128)} %broadcast_multiply_fusion.4) | copy-start | bytes 388
  757.6 188.6 %all-to-all-start.4 = ((f16[32,2,16,32,128]{4,3,2,1,0:T(8,128)(2,1)}), f16[32,2,16,32,128]{4,3,2,1,0:T(8,128)(2,1)}, u32[]{:S(2)}, u32[]{:S(2)}) async-start(f16[32,2,16,32,128]{4,3,2,1,0:T(8,128)(2,1)} %fusion.14), calls=%async_computation.4 | async-start | bytes 16777216 | tf_op jit(solution)/shard_map/all_to_all | solution.py:121
  946.2 223.6 %all-to-all-start.6 = ((f16[32,2,16,32,128]{4,3,2,1,0:T(8,128)(2,1)}), f16[32,2,16,32,128]{4,3,2,1,0:T(8,128)(2,1)}, u32[]{:S(2)}, u32[]{:S(2)}) async-start(f16[32,2,16,32,128]{4,3,2,1,0:T(8,128)(2,1)} %fusion.15), calls=%async_computation.6 | async-start | bytes 16777216 | tf_op jit(solution)/shard_map/all_to_all | solution.py:121
  1169.8 16.4 %copy-start.6 = (f32[32,16,32]{2,1,0:T(8,128)S(1)}, f32[32,16,32]{2,1,0:T(8,128)}, u32[]{:S(2)}) copy-start(f32[32,16,32]{2,1,0:T(8,128)} %copy-done.5) | copy-start | bytes 196612
  1169.8 16.4 %copy-start.8 = (f32[32,16,32]{2,1,0:T(8,128)S(1)}, f32[32,16,32]{2,1,0:T(8,128)}, u32[]{:S(2)}) copy-start(f32[32,16,32]{2,1,0:T(8,128)} %copy-done.7) | copy-start | bytes 196612
  1169.8 16.4 %copy-start.10 = (f32[32,16,32]{2,1,0:T(8,128)S(1)}, f32[32,16,32]{2,1,0:T(8,128)}, u32[]{:S(2)}) copy-start(f32[32,16,32]{2,1,0:T(8,128)} %copy-done.9) | copy-start | bytes 196612
  1169.8 16.4 %copy-start.12 = (f32[32,16,32]{2,1,0:T(8,128)S(1)}, f32[32,16,32]{2,1,0:T(8,128)}, u32[]{:S(2)}) copy-start(f32[32,16,32]{2,1,0:T(8,128)} %copy-done.11) | copy-start | bytes 196612
  1249.5 51.8 %all-to-all-start.5 = ((f16[4,256,16,128]{3,1,2,0:T(8,128)(2,1)}), f16[4,256,16,128]{3,1,2,0:T(8,128)(2,1)}, u32[]{:S(2)}, u32[]{:S(2)}) async-start(f16[4,256,16,128]{3,1,2,0:T(8,128)(2,1)} %copy.59), calls=%async_computation.5 | async-start | bytes 8388608 | tf_op jit(solution)/shard_map/all_to_all | solution.py:130
  1293.8 12.4 copy-start.15
  1301.3 65.1 %all-to-all-start.7 = ((f16[4,256,16,128]{3,1,2,0:T(8,128)(2,1)}), f16[4,256,16,128]{3,1,2,0:T(8,128)(2,1)}, u32[]{:S(2)}, u32[]{:S(2)}) async-start(f16[4,256,16,128]{3,1,2,0:T(8,128)(2,1)} %copy.65), calls=%async_computation.7 | async-start | bytes 8388608 | tf_op jit(solution)/shard_map/all_to_all | solution.py:130
  1366.4 18.2 %slice-start = ((s8[8388608]{0:T(1024)(128)(4,1)}), s8[4194304]{0:T(1024)(128)(4,1)S(1)}, s32[]{:S(2)}) async-start(s8[8388608]{0:T(1024)(128)(4,1)} %bitcast.170), calls=%async_computation.8 | async-start | bytes 8388608
  1377.0 7.6 slice-start.1
  1377.0 7.6 copy-start.14

commit v2 on v1

--- a/solution.py
+++ b/solution.py
@@ -92,16 +92,15 @@
         twists.append((c, s))
 
     row_parts = [row_matrix(chunk) for chunk in range(chunk_count)]
+    first_top = lax.pmax(bound_of(value), both) * float(grid_rows)
     frequencies = None
     for chunk in range(chunk_count):
         spectrum = contract("diap,pwz->diwaz", col_matrix, columns[chunk].astype(jnp.float32))
         c, s = twists[chunk]
         real, imag = spectrum[:, 0], spectrum[:, 1]
         spectrum = jnp.stack([real * c + imag * s, imag * c - real * s], axis=1)
-        largest = bound_of(columns[chunk]) * float(grid_rows)
-        every = lax.all_gather(largest, both)
-        arrived = lax.all_to_all(encode(spectrum, largest), both, 0, 0, tiled=True)
-        arrived = decode(arrived, every[:, None, None, None, None])
+        arrived = lax.all_to_all(encode(spectrum, first_top), both, 0, 0, tiled=True)
+        arrived = decode(arrived, first_top)
         term = contract("oksiw,siwaz->okaz", row_parts[chunk], arrived)
         frequencies = term if frequencies is None else frequencies + term
 
@@ -113,22 +112,23 @@
         ]
     )
 
+    largest = bound_of(filtered)
+    norms = jnp.sum(jnp.square(filtered * (1.0 / largest)), axis=(0, 1))
+    second_top = lax.pmax(largest * jnp.sqrt(jnp.max(norms) * grid_cols), both)
+    second_top = jnp.maximum(second_top, 1e-30)
+    last_top = second_top * (float(grid_rows) / period)
     settled = []
     for chunk in range(chunk_count):
         leaving = contract("oksiw,okaz->siwaz", row_parts[chunk], filtered)
-        largest = bound_of(leaving)
-        every = lax.all_gather(largest, both)
-        returned = lax.all_to_all(encode(leaving, largest), both, 0, 0, tiled=True)
-        returned = decode(returned, every[:, None, None, None, None] * (1.0 / period))
+        returned = lax.all_to_all(encode(leaving, second_top), both, 0, 0, tiled=True)
+        returned = decode(returned, second_top * (1.0 / period))
         c, s = twists[chunk]
         real, imag = returned[:, 0], returned[:, 1]
         returned = jnp.stack([real * c - imag * s, imag * c + real * s], axis=1)
         convolved = contract("diap,diwaz->pwz", col_matrix, returned)
-        largest = bound_of(convolved)
-        every = lax.all_gather(largest, "row")
-        coded = encode(convolved, largest).reshape(row_count, local_rows, width, channels)
+        coded = encode(convolved, last_top).reshape(row_count, local_rows, width, channels)
         coded = lax.all_to_all(coded, "row", 0, 0, tiled=True)
-        settled.append(decode(coded, every[:, None, None, None]))
+        settled.append(decode(coded, last_top))
     settled = jnp.stack(settled, axis=1)
     settled = settled.transpose(2, 0, 1, 3, 4).reshape(local_rows, local_cols, channels)
     result = gate.astype(jnp.float32) * (settled + skip * value.astype(jnp.float32))

time: 1400 us -> 1410 us (level)
  waiting for transfers between devices: 219 us -> 561 us
  blocking collectives: 417 us -> 113 us
  matrix products: 396 us -> 368 us
    unnamed x3 -> x0, blocking collectives: 417 us -> none
    all_to_all x4, waiting for transfers between devices: 188 us -> 509 us  [the longest x2 280 us: convolve(): lax.all_to_all(encode(leaving, second_top), both, 0, 0, tiled=True)]
    pmax x0 -> x2, blocking collectives: none -> 113 us  [the longest x1 76.6 us: convolve(): first_top = lax.pmax(bound_of(value), both) * float(grid_rows)]
    all_to_all x2, waiting for transfers between devices: 4.39 us -> 48.6 us  [convolve(): coded = lax.all_to_all(coded, 'row', 0, 0, tiled=True)]
    dot_general x8, matrix products: 396 us -> 368 us  [contract(): jnp.einsum(spec, left, right, precision=lax.Precision.HIGH, preferred_ele...]
    another operation x1 -> x2, other arithmetic: 34 us -> 57.8 us  [convolve(): jnp.stack([real * filter_real - imag * filter_imag, real * filter_imag +...]
    all_to_all x2, waiting for transfers between devices: 26.4 us -> 3.11 us  [convolve(): lax.all_to_all(pieces[:, :, chunk], 'row', split_axis=1, concat_axis=0, t...]
    convert_element_type x6 -> x4, other arithmetic: 46.8 us -> 34.8 us  [encode(): return (scaled * jnp.abs(scaled)).astype(jnp.float16)]
  transfers between devices with their start and end apart: 8 -> 8, of which waited for: 5 -> 7; matrix products, arithmetic and copies ran while one was open for 28% -> 25% of each run, Pallas kernels for 0% -> 0%
where the time goes in v2:
time: 1410 us
  waiting for transfers between devices  561 us (40%)
  matrix products  368 us (26%)
  other arithmetic  293 us (21%)
  blocking collectives  113 us (8%)
  starting transfers between devices  37.2 us (3%)
  local copies, waits for them, and re-layouts  31.8 us (2%)
    dot_general x8, matrix products, contract(): jnp.einsum(spec, left, right, precision=lax.Precision.HIGH, preferred_ele...  368 us
    all_to_all x2, waiting for transfers between devices, convolve(): lax.all_to_all(encode(leaving, second_top), both, 0, 0, tiled=True)  280 us
    all_to_all x2, waiting for transfers between devices, convolve(): lax.all_to_all(encode(spectrum, first_top), both, 0, 0, tiled=True)  229 us
    pmax x1, blocking collectives, convolve(): first_top = lax.pmax(bound_of(value), both) * float(grid_rows)  76.6 us
    select_n x4, other arithmetic, decode(): return jnp.where(wide < 0.0, -root, root)  64.8 us
    another operation x2, other arithmetic, convolve(): jnp.stack([real * filter_real - imag * filter_imag, real * filter_imag +...  57.8 us
    all_to_all x2, waiting for transfers between devices, convolve(): coded = lax.all_to_all(coded, 'row', 0, 0, tiled=True)  48.6 us
    pmax x1, blocking collectives, convolve(): second_top = lax.pmax(largest * jnp.sqrt(jnp.max(norms) * grid_cols), both)  36.9 us
  transfers between devices with their start and end apart: 8, of which 7 were waited for; matrix products, arithmetic and copies ran while one was open for 25% of the time, Pallas kernels for 0%

profile of v2, /device:TPU:0, one launch (start us, length us, event | category | flops | bytes accessed | tf_op | source)
XLA Modules:
  0.0 1408.6 jit_solution(15411634138283325062)
XLA Ops:
  0.0 5.8 slice_bitcast_fusion.2
  5.8 4.7 copy.68
  10.5 5.2 all-to-all-start
  15.7 5.9 abs_reduce_fusion.1
  22.3 76.6 %pmax.14 = f32[]{:T(128)} all-reduce(f32[]{:T(128)S(6)} %max.13), channel_id=1, replica_groups=mesh['row'=4,'col'=8] {'row','col'}, use_global_device_ids=true, to_apply=%region_1.2 | all-reduce | flops 1 | bytes 8 | tf_op jit(solution)/shard_map/pmax | solution.py:95
  98.8 6.9 copy.71
  106.4 2.1 fusion.100
  108.5 0.0 copy-start.9
  108.5 0.0 copy-start.11
  108.6 19.0 %fusion.84 = (f32[32,1,32,1024]{3,2,1,0:T(8,128)}, f32[32,1,32,1024]{3,2,1,0:T(8,128)}) fusion(s32[32,32]{1,0:T(8,128)S(1)} %multiply_add_fusion.4), kind=kLoop, calls=%fused_computation.138 | loop fusion | flops 15728640 | bytes 8392704 | tf_op jit(solution)/shard_map/cos | solution.py:15
  127.5 0.0 all-to-all-done
  127.5 5.2 all-to-all-start.2
  132.8 2.6 copy.69
  135.4 0.8 copy-done.1
  136.2 1.3 copy-done.3
  137.5 28.5 %convolution_bitcast_fusion.1 = f32[32,2,16,32,128]{4,3,2,1,0:T(8,128)S(1)} fusion(bf16[1024,16,128,1,1]{2,0,1,4,3:T(8,128)(2,1)S(1)} %bitcast.157, f32[32,1,32,1024]{3,2,1,0:T(8,128)S(1)} %copy-done.3, f32[32,1,32,1024]{3,2,1,0:T(8,128)S(1)} %copy-done.1), kind=kOutput, calls=%fused_computation.71 | convolution fusion | flops 25771900928 | bytes 29360128 | tf_op jit(solution)/shard_map/diap,pwz->diwaz/dot_general | solution.py:19
  166.0 5.6 multiply_add_fusion.3
  171.6 4.8 fusion.13
  176.4 3.1 all-to-all-done.2
  179.5 3.7 all-to-all-start.1
  183.9 8.4 fusion.87
  192.3 4.3 maximum_bitcast_fusion.2
  196.6 8.8 fusion.89
  205.5 4.2 maximum_bitcast_fusion
  209.7 2.6 copy.72
  212.3 0.8 copy-done.4
  213.1 17.9 %convolution_bitcast_fusion = f32[32,2,16,32,128]{4,3,2,1,0:T(8,128)S(1)} fusion(bf16[1024,16,128,1,1]{2,0,1,4,3:T(8,128)(2,1)S(1)} %bitcast.159, f32[32,1,32,1024]{3,2,1,0:T(8,128)S(1)} %copy-done.4, f32[32,1,32,1024]{3,2,1,0:T(8,128)S(1)} %copy-done.2), kind=kOutput, calls=%fused_computation.70 | convolution fusion | flops 25771900928 | bytes 29360128 | tf_op jit(solution)/shard_map/diap,pwz->diwaz/dot_general | solution.py:19
  231.0 5.6 multiply_add_fusion.2
  236.7 4.8 fusion.14
  241.5 126.6 %all-to-all-done.1 = f16[32,2,16,32,128]{4,3,2,1,0:T(8,128)(2,1)} async-done(((f16[32,2,16,32,128]{4,3,2,1,0:T(8,128)(2,1)}), f16[32,2,16,32,128]{4,3,2,1,0:T(8,128)(2,1)}, u32[]{:S(2)}, u32[]{:S(2)}) %all-to-all-start.1) | async-done | bytes 8388640 | tf_op jit(solution)/shard_map/all_to_all | solution.py:102
  368.1 3.7 all-to-all-start.3
  371.8 16.3 %negate_select_fusion.3 = f32[32,2,16,32,128]{4,3,2,1,0:T(8,128)} fusion(f16[32,2,16,32,128]{4,3,2,1,0:T(8,128)(2,1)} %all-to-all-done.1, f32[]{:T(128)S(6)} %mul.600), kind=kLoop, calls=%fused_computation.14 | loop fusion | flops 25165824 | bytes 25165828 | tf_op jit(solution)/shard_map/jit(_where)/select_n | solution.py:32
  388.1 66.3 %fusion.28 = f32[2,1024,32,128,1,1]{3,1,5,4,2,0:T(8,128)} fusion(f32[32,2,16,32,128]{4,3,2,1,0:T(8,128)} %negate_select_fusion.3, f32[1,1024,32,2,16]{1,2,4,3,0:T(8,128)} %get-tuple-element.22, f32[1,1024,32,2,16]{1,2,4,3,0:T(8,128)S(1)} %copy-done), kind=kOutput, calls=%fused_computation.56 | convolution fusion | flops 51541704704 | bytes 58720256 | tf_op jit(solution)/shard_map/oksiw,siwaz->okaz/dot_general | solution.py:19
  454.3 102.4 %all-to-all-done.3 = f16[32,2,16,32,128]{4,3,2,1,0:T(8,128)(2,1)} async-done(((f16[32,2,16,32,128]{4,3,2,1,0:T(8,128)(2,1)}), f16[32,2,16,32,128]{4,3,2,1,0:T(8,128)(2,1)}, u32[]{:S(2)}, u32[]{:S(2)}) %all-to-all-start.3) | async-done | bytes 8388640 | tf_op jit(solution)/shard_map/all_to_all | solution.py:102
  556.7 16.1 %negate_select_fusion.2 = f32[32,2,16,32,128]{4,3,2,1,0:T(8,128)} fusion(f16[32,2,16,32,128]{4,3,2,1,0:T(8,128)(2,1)} %all-to-all-done.3, f32[]{:T(128)S(6)} %mul.600), kind=kLoop, calls=%fused_computation.12 | loop fusion | flops 25165824 | bytes 25165828 | tf_op jit(solution)/shard_map/jit(_where)/select_n | solution.py:32
  572.8 68.7 %bitcast_add_fusion = f32[2,1024,32,128]{3,1,2,0:T(8,128)} fusion(f32[2,1024,32,128,1,1]{3,1,5,4,2,0:T(8,128)} %fusion.28, f32[32,2,16,32,128]{4,3,2,1,0:T(8,128)} %negate_select_fusion.2, f32[1,1024,32,2,16]{1,2,4,3,0:T(8,128)} %get-tuple-element.20, f32[1,1024,32,2,16]{1,2,4,3,0:T(8,128)} %get-tuple-element.19), kind=kOutput, calls=%fused_computation.1 | convolution fusion | flops 51550093312 | bytes 92274688 | tf_op jit(solution)/shard_map/oksiw,siwaz->okaz/dot_general | solution.py:19
  641.5 33.8 %subtract_bitcast_fusion = (f32[1,1024,32,128]{3,1,2,0:T(8,128)}, f32[1,1024,32,128]{3,1,2,0:T(8,128)}) fusion(f32[2,1024,32,128]{3,1,2,0:T(8,128)} %bitcast_add_fusion, f32[1024,32,128]{2,1,0:T(8,128)} %param.8, f32[1024,32,128]{2,1,0:T(8,128)} %param.7), kind=kLoop, calls=%fused_computation.61 | loop fusion | flops 25165824 | bytes 100663296 | tf_op jit(solution)/shard_map/stack | solution.py:108
  675.4 24.0 %fusion.4 = (f32[2,1024,32,128,1,1]{3,1,2,0,5,4:T(8,128)}, f32[]{:T(128)}) fusion(f32[1,1024,32,128]{3,1,2,0:T(8,128)} %get-tuple-element.6, f32[1,1024,32,128]{3,1,2,0:T(8,128)} %get-tuple-element.5), kind=kLoop, calls=%fused_computation.16 | loop fusion | flops 25165824 | bytes 67108864 | tf_op jit(solution)/shard_map/stack | solution.py:108
  700.0 12.5 multiply_reduce_fusion
  712.6 0.6 reduce_max.29
  713.9 36.9 %pmax.15 = f32[]{:T(128)} all-reduce(f32[]{:T(128)S(6)} %mul.626), channel_id=1, replica_groups=mesh['row'=4,'col'=8] {'row','col'}, use_global_device_ids=true, to_apply=%region_5.6 | all-reduce | flops 1 | bytes 8 | tf_op jit(solution)/shard_map/pmax | solution.py:117
  751.5 60.7 %fusion.50 = f32[32,2,16,32,128]{4,0,3,2,1:T(8,128)} fusion(f32[2,1024,32,128,1,1]{3,1,2,0,5,4:T(8,128)} %get-tuple-element.7, f32[1,1024,32,2,16]{1,2,4,3,0:T(8,128)} %get-tuple-element.22, f32[1,1024,32,2,16]{1,2,4,3,0:T(8,128)} %get-tuple-element.21), kind=kOutput, calls=%fused_computation.104 | convolution fusion | flops 51541704704 | bytes 58720256 | tf_op jit(solution)/shard_map/oksiw,okaz->siwaz/dot_general | solution.py:19
  812.2 12.7 fusion.15
  824.9 5.3 all-to-all-start.4
  830.3 60.7 %fusion.55 = f32[32,2,16,32,128]{4,0,3,2,1:T(8,128)} fusion(f32[2,1024,32,128,1,1]{3,1,2,0,5,4:T(8,128)} %get-tuple-element.7, f32[1,1024,32,2,16]{1,2,4,3,0:T(8,128)} %get-tuple-element.20, f32[1,1024,32,2,16]{1,2,4,3,0:T(8,128)} %get-tuple-element.19), kind=kOutput, calls=%fused_computation.105 | convolution fusion | flops 51541704704 | bytes 58720256 | tf_op jit(solution)/shard_map/oksiw,okaz->siwaz/dot_general | solution.py:19
  891.0 12.5 fusion.16
  903.5 111.6 %all-to-all-done.4 = f16[32,2,16,32,128]{4,3,2,1,0:T(8,128)(2,1)} async-done(((f16[32,2,16,32,128]{4,3,2,1,0:T(8,128)(2,1)}), f16[32,2,16,32,128]{4,3,2,1,0:T(8,128)(2,1)}, u32[]{:S(2)}, u32[]{:S(2)}) %all-to-all-start.4) | async-done | bytes 8388640 | tf_op jit(solution)/shard_map/all_to_all | solution.py:123
  1015.2 3.7 all-to-all-start.6
  1018.9 16.1 %negate_select_fusion.1 = f32[32,2,16,32,128]{4,3,2,1,0:T(8,128)} fusion(f16[32,2,16,32,128]{4,3,2,1,0:T(8,128)(2,1)} %all-to-all-done.4, f32[]{:T(128)S(6)} %mul.630), kind=kLoop, calls=%fused_computation.10 | loop fusion | flops 25165824 | bytes 25165828 | tf_op jit(solution)/shard_map/jit(_where)/select_n | solution.py:32
  1035.0 168.7 %all-to-all-done.6 = f16[32,2,16,32,128]{4,3,2,1,0:T(8,128)(2,1)} async-done(((f16[32,2,16,32,128]{4,3,2,1,0:T(8,128)(2,1)}), f16[32,2,16,32,128]{4,3,2,1,0:T(8,128)(2,1)}, u32[]{:S(2)}, u32[]{:S(2)}) %all-to-all-start.6) | async-done | bytes 8388640 | tf_op jit(solution)/shard_map/all_to_all | solution.py:123
  1203.8 16.3 %negate_select_fusion = f32[32,2,16,32,128]{4,3,2,1,0:T(8,128)} fusion(f16[32,2,16,32,128]{4,3,2,1,0:T(8,128)(2,1)} %all-to-all-done.6, f32[]{:T(128)S(6)} %mul.630), kind=kLoop, calls=%fused_computation.8 | loop fusion | flops 25165824 | bytes 25165828 | tf_op jit(solution)/shard_map/jit(_where)/select_n | solution.py:32
  1220.1 20.2 %multiply_subtract_fusion = (f32[32,1,16,32,128]{4,3,2,1,0:T(8,128)}, f32[32,1,16,32,128]{4,3,2,1,0:T(8,128)}, f32[32,1,16,32,128]{4,3,2,1,0:T(8,128)S(1)}, f32[32,1,16,32,128]{4,3,2,1,0:T(8,128)}) fusion(f32[32,2,16,32,128]{4,3,2,1,0:T(8,128)} %negate_select_fusion, f32[32,16,32]{2,1,0:T(8,128)S(1)} %copy-done.8, f32[32,16,32]{2,1,0:T(8,128)S(1)} %copy-done.6, ...), kind=kLoop, calls=%fused_computation.94 | loop fusion | flops 25165824 | bytes 67371008 | tf_op jit(solution)/shard_map/sub | solution.py:127
  1240.3 32.8 %fusion.36 = f16[1024,16,128]{2,0,1:T(8,128)(2,1)S(1)} fusion(f32[]{:T(128)S(6)} %div.44, f32[32,1,16,32,128]{4,3,2,1,0:T(8,128)S(1)} %get-tuple-element.37, f32[32,1,16,32,128]{4,3,2,1,0:T(8,128)} %get-tuple-element.38, f32[32,1,32,1024]{3,2,1,0:T(8,128)} %get-tuple-element.30, f32[32,1,32,1024]{3,2,1,0:T(8,128)} %get-tuple-element.29), kind=kOutput, calls=%fused_computation.76 | convolution fusion | flops 25784483840 | bytes 29360132 | tf_op jit(solution)/shard_map/diap,diwaz->pwz/dot_general | solution.py:19
  1273.1 3.0 copy.82
  1276.1 5.3 all-to-all-start.5
  1281.5 32.3 %fusion.38 = f16[1024,16,128]{2,0,1:T(8,128)(2,1)S(1)} fusion(f32[]{:T(128)S(6)} %div.44, f32[32,1,16,32,128]{4,3,2,1,0:T(8,128)} %get-tuple-element.12, f32[32,1,16,32,128]{4,3,2,1,0:T(8,128)} %get-tuple-element.11, f32[32,1,32,1024]{3,2,1,0:T(8,128)} %get-tuple-element.30, f32[32,1,32,1024]{3,2,1,0:T(8,128)} %get-tuple-element.29), kind=kOutput, calls=%fused_computation.78 | convolution fusion | flops 25784483840 | bytes 29360132 | tf_op jit(solution)/shard_map/diap,diwaz->pwz/dot_general | solution.py:19
  1313.8 3.1 copy.88
  1316.9 12.1 all-to-all-done.5
  1329.0 5.1 all-to-all-start.7
  1334.0 10.3 fusion.37
  1344.4 36.6 %all-to-all-done.7 = f16[4,256,16,128]{3,1,2,0:T(8,128)(2,1)} async-done(((f16[4,256,16,128]{3,1,2,0:T(8,128)(2,1)}), f16[4,256,16,128]{3,1,2,0:T(8,128)(2,1)}, u32[]{:S(2)}, u32[]{:S(2)}) %all-to-all-start.7) | async-done | bytes 4194336 | tf_op jit(solution)/shard_map/all_to_all | solution.py:130
  1380.9 10.6 fusion.39
  1391.5 7.6 pad_maximum_fusion.1
  1399.2 9.2 fusion.26
  (35 shorter events, 0.1 us)
Async XLA Ops:
  10.5 117.0 %all-to-all-start = ((bf16[256,4,16,128]{3,0,2,1:T(8,128)(2,1)}), bf16[256,4,16,128]{3,0,2,1:T(8,128)(2,1)}, u32[]{:S(2)}, u32[]{:S(2)}) async-start(bf16[256,4,16,128]{3,0,2,1:T(8,128)(2,1)} %copy.68), calls=%async_computation | async-start | bytes 8388608 | tf_op jit(solution)/shard_map/all_to_all | solution.py:67
  108.5 57.5 %copy-start.9 = (f32[32,16,32]{2,1,0:T(8,128)}, f32[32,16,32]{2,1,0:T(8,128)S(1)}, u32[]{:S(2)}) copy-start(f32[32,16,32]{2,1,0:T(8,128)S(1)} %get-tuple-element.27) | copy-start | bytes 196612
  108.5 57.5 %copy-start.11 = (f32[32,16,32]{2,1,0:T(8,128)}, f32[32,16,32]{2,1,0:T(8,128)S(1)}, u32[]{:S(2)}) copy-start(f32[32,16,32]{2,1,0:T(8,128)S(1)} %get-tuple-element.28) | copy-start | bytes 196612
  108.5 122.5 %copy-start.5 = (f32[32,16,32]{2,1,0:T(8,128)}, f32[32,16,32]{2,1,0:T(8,128)S(1)}, u32[]{:S(2)}) copy-start(f32[32,16,32]{2,1,0:T(8,128)S(1)} %get-tuple-element.23) | copy-start | bytes 196612
  108.6 122.5 %copy-start.7 = (f32[32,16,32]{2,1,0:T(8,128)}, f32[32,16,32]{2,1,0:T(8,128)S(1)}, u32[]{:S(2)}) copy-start(f32[32,16,32]{2,1,0:T(8,128)S(1)} %get-tuple-element.24) | copy-start | bytes 196612
  127.5 52.0 %all-to-all-start.2 = ((bf16[256,4,16,128]{3,0,2,1:T(8,128)(2,1)}), bf16[256,4,16,128]{3,0,2,1:T(8,128)(2,1)}, u32[]{:S(2)}, u32[]{:S(2)}) async-start(bf16[256,4,16,128]{3,0,2,1:T(8,128)(2,1)} %copy.71), calls=%async_computation.2 | async-start | bytes 8388608 | tf_op jit(solution)/shard_map/all_to_all | solution.py:67
  132.7 3.5 copy-start.1
  132.8 4.7 copy-start.3
  179.5 188.6 %all-to-all-start.1 = ((f16[32,2,16,32,128]{4,3,2,1,0:T(8,128)(2,1)}), f16[32,2,16,32,128]{4,3,2,1,0:T(8,128)(2,1)}, u32[]{:S(2)}, u32[]{:S(2)}) async-start(f16[32,2,16,32,128]{4,3,2,1,0:T(8,128)(2,1)} %fusion.13), calls=%async_computation.1 | async-start | bytes 16777216 | tf_op jit(solution)/shard_map/all_to_all | solution.py:102
  205.4 6.9 copy-start.2
  209.7 3.4 copy-start.4
  368.1 188.6 %all-to-all-start.3 = ((f16[32,2,16,32,128]{4,3,2,1,0:T(8,128)(2,1)}), f16[32,2,16,32,128]{4,3,2,1,0:T(8,128)(2,1)}, u32[]{:S(2)}, u32[]{:S(2)}) async-start(f16[32,2,16,32,128]{4,3,2,1,0:T(8,128)(2,1)} %fusion.14), calls=%async_computation.3 | async-start | bytes 16777216 | tf_op jit(solution)/shard_map/all_to_all | solution.py:102
  371.8 16.3 %copy-start = (f32[1,1024,32,2,16]{1,2,4,3,0:T(8,128)S(1)}, f32[1,1024,32,2,16]{1,2,4,3,0:T(8,128)}, u32[]{:S(2)}) copy-start(f32[1,1024,32,2,16]{1,2,4,3,0:T(8,128)} %get-tuple-element.21) | copy-start | bytes 12582916
  824.9 190.3 %all-to-all-start.4 = ((f16[32,2,16,32,128]{4,3,2,1,0:T(8,128)(2,1)}), f16[32,2,16,32,128]{4,3,2,1,0:T(8,128)(2,1)}, u32[]{:S(2)}, u32[]{:S(2)}) async-start(f16[32,2,16,32,128]{4,3,2,1,0:T(8,128)(2,1)} %fusion.15), calls=%async_computation.4 | async-start | bytes 16777216 | tf_op jit(solution)/shard_map/all_to_all | solution.py:123
  1015.2 188.6 %all-to-all-start.6 = ((f16[32,2,16,32,128]{4,3,2,1,0:T(8,128)(2,1)}), f16[32,2,16,32,128]{4,3,2,1,0:T(8,128)(2,1)}, u32[]{:S(2)}, u32[]{:S(2)}) async-start(f16[32,2,16,32,128]{4,3,2,1,0:T(8,128)(2,1)} %fusion.16), calls=%async_computation.6 | async-start | bytes 16777216 | tf_op jit(solution)/shard_map/all_to_all | solution.py:123
  1035.0 185.1 %copy-start.6 = (f32[32,16,32]{2,1,0:T(8,128)S(1)}, f32[32,16,32]{2,1,0:T(8,128)}, u32[]{:S(2)}) copy-start(f32[32,16,32]{2,1,0:T(8,128)} %copy-done.5) | copy-start | bytes 196612
  1035.0 185.1 %copy-start.8 = (f32[32,16,32]{2,1,0:T(8,128)S(1)}, f32[32,16,32]{2,1,0:T(8,128)}, u32[]{:S(2)}) copy-start(f32[32,16,32]{2,1,0:T(8,128)} %copy-done.7) | copy-start | bytes 196612
  1035.0 185.1 %copy-start.10 = (f32[32,16,32]{2,1,0:T(8,128)S(1)}, f32[32,16,32]{2,1,0:T(8,128)}, u32[]{:S(2)}) copy-start(f32[32,16,32]{2,1,0:T(8,128)} %copy-done.9) | copy-start | bytes 196612
  1035.0 185.1 %copy-start.12 = (f32[32,16,32]{2,1,0:T(8,128)S(1)}, f32[32,16,32]{2,1,0:T(8,128)}, u32[]{:S(2)}) copy-start(f32[32,16,32]{2,1,0:T(8,128)} %copy-done.11) | copy-start | bytes 196612
  1276.1 52.8 %all-to-all-start.5 = ((f16[4,256,16,128]{3,1,2,0:T(8,128)(2,1)}), f16[4,256,16,128]{3,1,2,0:T(8,128)(2,1)}, u32[]{:S(2)}, u32[]{:S(2)}) async-start(f16[4,256,16,128]{3,1,2,0:T(8,128)(2,1)} %copy.82), calls=%async_computation.5 | async-start | bytes 8388608 | tf_op jit(solution)/shard_map/all_to_all | solution.py:130
  1329.0 52.0 %all-to-all-start.7 = ((f16[4,256,16,128]{3,1,2,0:T(8,128)(2,1)}), f16[4,256,16,128]{3,1,2,0:T(8,128)(2,1)}, u32[]{:S(2)}, u32[]{:S(2)}) async-start(f16[4,256,16,128]{3,1,2,0:T(8,128)(2,1)} %copy.88), calls=%async_computation.7 | async-start | bytes 8388608 | tf_op jit(solution)/shard_map/all_to_all | solution.py:130
  1380.9 18.2 %slice-start = ((s8[8388608]{0:T(1024)(128)(4,1)}), s8[4194304]{0:T(1024)(128)(4,1)S(1)}, s32[]{:S(2)}) async-start(s8[8388608]{0:T(1024)(128)(4,1)} %bitcast.154), calls=%async_computation.8 | async-start | bytes 8388608
  1391.5 7.6 slice-start.1
  1391.5 7.6 copy-start.13
